TPU v7x, 128 devices: a whole 4x4x4 slice. The times are simulated.
128 devices in a mesh: lead: 4 (over x_lo, core), space: 32 (over z, y, x_hi).
Axes of the slice: x: 4 (x_hi: 2, x_lo: 2; x = x_hi * 2 + x_lo), y: 4, z: 4, core: 2. Of those that a mesh axis runs over, the one named last changes fastest.
Arguments:
- latent: bfloat16 [4, 128, 256, 512], P('lead', 'space'), may hold values from -6 to 6
- lead_index: int32 [4], P('lead'), may hold values from 0 to 720
- conv_kernel: float32 [3, 3, 512], replicated, may hold values from -2.5 to 2.5
- cond_table: float32 [721, 2, 512], replicated, may hold values from -3 to 3
- w_qkv: bfloat16 [512, 1536], replicated, may hold values from -0.25 to 0.25
- w_out: bfloat16 [512, 512], replicated, may hold values from -0.25 to 0.25
- cotangent: bfloat16 [4, 128, 256, 512], P('lead', 'space'), may hold values from -6 to 6
Outputs:
- grad_x: bfloat16 [4, 128, 256, 512], P('lead', 'space')
- grad_qkv: float32 [512, 1536], replicated
- grad_out: float32 [512, 512], replicated
- grad_kernel: float32 [3, 3, 512], replicated
- grad_table: float32 [721, 2, 512], replicated
All inputs are finite; a program needn't handle non-finite values.
Results may differ from a plain program's by a relative error of at most 0.0095.
Values may be sent and summed in bfloat16 or wider, within the bound.
A program may use at most 128 MiB of HBM per device.

v0:
```python
import functools
import math

import jax
import jax.numpy as jnp
from jax import lax
from jax.experimental import pallas as pl
from jax.experimental.pallas import tpu as pltpu
from jax.sharding import PartitionSpec as P

HDIM = 32
GRID = 8
EPSILON = 1e-05
ROWS = 4
COLS = 256
D = 512
PEERS = 8
CHUNK = 32
MESH = pl.DeviceIdType.MESH
F32 = jnp.float32
BF16 = jnp.bfloat16
VMEM_LIMIT = 52 * 1024 * 1024


def remote(src, dst, send, recv, device):
    return pltpu.make_async_remote_copy(
        src_ref=src, dst_ref=dst, send_sem=send, recv_sem=recv, device_id=device, device_id_type=MESH
    )


def dot(a, b, ca, cb):
    return lax.dot_general(a, b, (((ca,), (cb,)), ((), ())), preferred_element_type=F32)


def send_order():
    p = lax.broadcasted_iota(jnp.int32, (COLS, COLS), 0)
    col = lax.broadcasted_iota(jnp.int32, (COLS, COLS), 1)
    return jnp.where((p & 7) * 32 + (p >> 5) * 4 + ((p >> 3) & 3) == col, 1.0, 0.0).astype(BF16)


def field_order():
    p = lax.broadcasted_iota(jnp.int32, (COLS, COLS), 1)
    col = lax.broadcasted_iota(jnp.int32, (COLS, COLS), 0)
    return jnp.where((p & 7) * 32 + (p >> 5) * 4 + ((p >> 3) & 3) == col, 1.0, 0.0).astype(BF16)


def group_order():
    g = lax.broadcasted_iota(jnp.int32, (COLS, COLS), 0)
    p = lax.broadcasted_iota(jnp.int32, (COLS, COLS), 1)
    return jnp.where(((g >> 3) & 7) * 32 + (g >> 6) * 8 + (g & 7) == p, 1.0, 0.0).astype(BF16)


def attention_row(x, c, wqkv, wout, xg, cg, qkv, da, att, dp, perm, i):
    scale = 1.0 / math.sqrt(HDIM)
    c2 = scale * math.log2(math.e)
    base = pl.multiple_of(i * COLS, COLS)
    here = pl.ds(base, COLS)
    gx = dot(perm[...], x, 1, 0).astype(BF16)
    gc = dot(perm[...], c, 1, 0).astype(BF16)
    xg[here, :] = gx
    cg[here, :] = gc
    for n in range(3):
        qkv[:, n * D : (n + 1) * D] = dot(gx, wqkv[:, n * D : (n + 1) * D], 1, 0).astype(BF16)
    da[...] = dot(gc, wout[...], 1, 1).astype(BF16)
    lane = lax.broadcasted_iota(jnp.int32, (1, 128), 1) // HDIM
    masks16 = [jnp.where(lane == h, 1.0, 0.0).astype(BF16) for h in range(4)]
    lanes = lax.broadcasted_iota(jnp.int32, (64, 128), 1) // HDIM
    picks = [lanes == h for h in range(3)]

    def spread(t):
        return jnp.concatenate([t * m for m in masks16], axis=0)

    def gather(t):
        total = jnp.where(picks[2], t[128:192], t[192:256])
        total = jnp.where(picks[1], t[64:128], total)
        return jnp.where(picks[0], t[0:64], total)

    def group(g, carry):
        rows = pl.ds(pl.multiple_of(g * 64, 64), 64)
        out = pl.ds(pl.multiple_of(base + g * 64, 64), 64)
        at = [(t * 128, t * 128 + 128) for t in range(4)]
        qs = [spread(qkv[rows, lo:hi]) for lo, hi in at]
        k = [qkv[rows, D + lo : D + hi] for lo, hi in at]
        v = [qkv[rows, 2 * D + lo : 2 * D + hi] for lo, hi in at]
        ds_ = [spread(da[rows, lo:hi]) for lo, hi in at]
        s = [dot(a, b, 1, 1) for a, b in zip(k, qs)]
        dpr = [dot(a, b, 1, 1) for a, b in zip(v, ds_)]
        m = [jnp.max(a, axis=0, keepdims=True) * c2 for a in s]
        e = [jnp.exp2(a * c2 - b) for a, b in zip(s, m)]
        p = [a * (1.0 / jnp.sum(a, axis=0, keepdims=True)) for a in e]
        p16 = [a.astype(BF16) for a in p]
        inner = [jnp.sum(a * b, axis=0, keepdims=True) for a, b in zip(p, dpr)]
        dsc = [(a * (b - c)).astype(BF16) for a, b, c in zip(p, dpr, inner)]
        o1 = [dot(a, b, 0, 0) for a, b in zip(p16, v)]
        o2 = [dot(a, b, 1, 0) for a, b in zip(p16, ds_)]
        o3 = [dot(a, b, 0, 0) for a, b in zip(dsc, k)]
        o4 = [dot(a, b, 1, 0) for a, b in zip(dsc, qs)]
        for n, (lo, hi) in enumerate(at):
            att[out, lo:hi] = gather(o1[n]).astype(BF16)
            dp[out, 2 * D + lo : 2 * D + hi] = o2[n].astype(BF16)
            dp[out, lo:hi] = (gather(o3[n]) * scale).astype(BF16)
            dp[out, D + lo : D + hi] = (o4[n] * scale).astype(BF16)
        return carry

    lax.fori_loop(0, 4, group, 0)


def normed_back(dp, wqkv, i):
    here = pl.ds(pl.multiple_of(i * COLS, COLS), COLS)
    dnf = dot(dp[here, :], wqkv[...], 1, 1)
    blocks = [dnf[g * 64 + m * 8 : g * 64 + m * 8 + 8] for m in range(8) for g in range(4)]
    return jnp.concatenate(blocks, axis=0).astype(BF16).reshape(PEERS, CHUNK, D)


def weight_grads(xg, cg, att, dp, grads, h):
    half = pl.ds(pl.multiple_of(h * 256, 256), 256)
    for n in range(3):
        grads[h, :, n * D : (n + 1) * D] = dot(xg[:, half], dp[:, n * D : (n + 1) * D], 0, 0).astype(BF16)
    grads[h, :, 3 * D :] = dot(att[:, half], cg[...], 0, 0).astype(BF16)


PARTS = ((0, 640, "xyz"), (640, 640, "yzx"), (1280, 768, "zxy"))


def section_kernel(
    latent_any, cot_any, ck, mod, wqkv_any, wout_any, leadrow,
    gx, total, small,
    latent, cot, wqkv, wout, halo, xp, dpad, nf, inv, nrm, fperm, gperm, bperm,
    xs, cs, xr, cr, xg, cg, qkv, da, att, dp, dn, dr, dnf, hsend, hrecv,
    grads, r0, a0, r1, a1, r2, ex, ksum, tsum, sm, s1, s2, s3, s4,
    lsem, hsem, xsem, csem, dsem, bsem, wsem, rsem, gsem, ssem,
):
    lead = lax.axis_index("lead")
    space = lax.axis_index("space")
    a, q = space // 4, lax.rem(space, 4)
    core, x_lo = lax.rem(lead, 2), lead // 2
    z, y, x_hi = space // 8, lax.rem(space // 2, 4), lax.rem(space, 2)
    x = x_hi * 2 + x_lo
    coord = {"x": x, "y": y, "z": z}

    def at_axis(axis, j):
        if axis == "x":
            return ((lax.rem(j, 2) * 2 + core), space - x_hi + j // 2)
        if axis == "y":
            return (lead, space + (j - y) * 2)
        return (lead, space + (j - z) * 8)

    def ahead(axis, d):
        return lax.rem(coord[axis] + d, 4)

    def behind(axis, d):
        return lax.rem(coord[axis] + 4 - d, 4)

    twin = (lead + 1 - 2 * core, space)
    has_low, has_high = space > 0, space < 31

    loads = [
        pltpu.make_async_copy(src, dst, lsem.at[n])
        for n, (src, dst) in enumerate(
            ((latent_any, latent), (cot_any, cot), (wqkv_any, wqkv), (wout_any, wout))
        )
    ]
    for load in loads:
        load.start()

    @pl.when(space == 0)
    def _():
        halo[0] = jnp.zeros((COLS, D), BF16)
        hrecv[0] = jnp.zeros((COLS, D), BF16)

    @pl.when(space == 31)
    def _():
        halo[1] = jnp.zeros((COLS, D), BF16)
        hrecv[1] = jnp.zeros((COLS, D), BF16)

    barrier = pltpu.get_barrier_semaphore()

    def greet(device):
        pl.semaphore_signal(barrier, inc=1, device_id=device, device_id_type=MESH)

    def greet_peer(d, c):
        greet((lead, 4 * lax.rem(a + d, PEERS) + q))
        return c

    lax.fori_loop(1, PEERS, greet_peer, 0)
    for axis in "xyz":
        for d in range(1, 4):
            greet(at_axis(axis, ahead(axis, d)))
    greet(twin)

    @pl.when(has_low)
    def _():
        greet((lead, space - 1))

    @pl.when(has_high)
    def _():
        greet((lead, space + 1))

    fperm[...] = send_order()
    gperm[...] = group_order()
    bperm[...] = field_order()
    xp[:, 0:8, :] = jnp.zeros((ROWS + 2, 8, D), F32)
    xp[:, COLS + 8 : COLS + 16, :] = jnp.zeros((ROWS + 2, 8, D), F32)
    dpad[:, 0:8, :] = jnp.zeros((ROWS + 2, 8, D), F32)
    dpad[:, COLS + 8 : COLS + 16, :] = jnp.zeros((ROWS + 2, 8, D), F32)
    ksum[...] = jnp.zeros((9, 8, D), F32)
    tsum[...] = jnp.zeros((2, 8, D), F32)
    loads[0].wait()
    loads[1].wait()
    pl.semaphore_wait(barrier, 17 + jnp.where(has_low, 1, 0) + jnp.where(has_high, 1, 0))

    def edge_start(low, high, sem):
        @pl.when(has_low)
        def _():
            if low is not None:
                remote(low[0], low[1].at[1], sem.at[0], sem.at[2], (lead, space - 1)).start()

        @pl.when(has_high)
        def _():
            if high is not None:
                remote(high[0], high[1].at[0], sem.at[1], sem.at[3], (lead, space + 1)).start()

    def edge_wait(first, last, dst, sem):
        @pl.when(has_low)
        def _():
            remote(first, dst.at[1], sem.at[0], sem.at[2], (lead, space - 1)).wait_send()
            remote(last, dst.at[0], sem.at[1], sem.at[3], (lead, space - 1)).wait_recv()

        @pl.when(has_high)
        def _():
            remote(last, dst.at[0], sem.at[1], sem.at[3], (lead, space + 1)).wait_send()
            remote(first, dst.at[1], sem.at[0], sem.at[2], (lead, space + 1)).wait_recv()

    edge_start((latent.at[0], halo), (latent.at[3], halo), hsem)

    def send(bufs, out, sem, r):
        def one(d, c):
            t = lax.rem(a + d, PEERS)
            remote(bufs.at[r, t], out.at[r, a], sem.at[0, r, d], sem.at[1, r, d], (lead, 4 * t + q)).start()
            return c

        lax.fori_loop(1, PEERS, one, 0)
        pltpu.make_async_copy(bufs.at[r, a], out.at[r, a], sem.at[0, r, 0]).start()

    def finish(bufs, out, sem, r):
        def one(d, c):
            t = lax.rem(a + d, PEERS)
            f = lax.rem(a + PEERS - d, PEERS)
            remote(bufs.at[r, t], out.at[r, f], sem.at[0, r, d], sem.at[1, r, d], (lead, 4 * t + q)).wait()
            return c

        lax.fori_loop(1, PEERS, one, 0)
        pltpu.make_async_copy(bufs.at[r, a], out.at[r, a], sem.at[0, r, 0]).wait()

    def cot_row(r):
        cs[r] = dot(fperm[...], cot[r], 1, 0).astype(BF16).reshape(PEERS, CHUNK, D)
        send(cs, cr, csem, r)

    def norm_row(r):
        def chunk(c, carry):
            at = pl.multiple_of(c * CHUNK, CHUNK)
            w = [xp[r + m, pl.ds(at, CHUNK + 16), :] for m in range(3)]
            k = [ck[m : m + 1, :] for m in range(9)]
            t = [k[j] * w[0] + k[3 + j] * w[1] + k[6 + j] * w[2] for j in range(3)]
            res = w[1][8 : CHUNK + 8] + (
                t[0][7 : CHUNK + 7] + t[1][8 : CHUNK + 8] + t[2][9 : CHUNK + 9]
            )
            cen = res - jnp.mean(res, axis=-1, keepdims=True)
            iv = lax.rsqrt(jnp.mean(cen * cen, axis=-1, keepdims=True) + EPSILON)
            n = cen * iv
            nf[r, pl.ds(at, CHUNK), :] = n
            inv[r, pl.ds(at, CHUNK), :] = jnp.broadcast_to(iv, (CHUNK, 128))
            nrm[pl.ds(at, CHUNK), :] = (n * (1.0 + mod[0:1, :]) + mod[1:2, :]).astype(BF16)
            return carry

        lax.fori_loop(0, COLS // CHUNK, chunk, 0)
        xs[r] = dot(fperm[...], nrm[...], 1, 0).astype(BF16).reshape(PEERS, CHUNK, D)
        send(xs, xr, xsem, r)

    def fold(t):
        total = t[0:8]
        for n in range(8, CHUNK, 8):
            total = total + t[n : n + 8]
        return total

    def back_row(r):
        finish(dn, dr, dsem, r)
        dnf[...] = dot(bperm[...], dr[r].reshape(COLS, D), 1, 0)

        def chunk(c, carry):
            at = pl.multiple_of(c * CHUNK, CHUNK)
            here = pl.ds(at, CHUNK)
            dv = dnf[here, :]
            n = nf[r, here, :]
            iv = inv[r, here, 0:1]
            tsum[0] += fold(dv * n)
            tsum[1] += fold(dv)
            g = dv * (1.0 + mod[0:1, :])
            m1 = jnp.mean(g, axis=-1, keepdims=True)
            m2 = jnp.mean(g * n, axis=-1, keepdims=True)
            res = cot[r, here, :].astype(F32) + iv * (g - m1 - n * m2)
            dpad[r + 1, pl.ds(at + 8, CHUNK), :] = res
            return carry

        lax.fori_loop(0, COLS // CHUNK, chunk, 0)

    def kernel_rows(first, last):
        def chunk(i, carry):
            r = i // (COLS // CHUNK)
            at = pl.multiple_of(lax.rem(i, COLS // CHUNK) * CHUNK, CHUNK)
            w = dpad[r + 1, pl.ds(at, CHUNK + 16), :]
            dj = [w[9 - j : 9 - j + CHUNK] for j in range(3)]
            for m in range(3):
                xw = xp[r + m, pl.ds(at + 8, CHUNK), :]
                for j in range(3):
                    ksum[3 * m + j] += fold(xw * dj[j])
            return carry

        lax.fori_loop(first * (COLS // CHUNK), last * (COLS // CHUNK), chunk, 0)

    def out_row(r):
        def chunk(c, carry):
            at = pl.multiple_of(c * CHUNK, CHUNK)
            w = [dpad[r + m, pl.ds(at, CHUNK + 16), :] for m in range(3)]
            k = [ck[m : m + 1, :] for m in range(9)]
            t = [k[8 - j] * w[0] + k[5 - j] * w[1] + k[2 - j] * w[2] for j in range(3)]
            res = w[1][8 : CHUNK + 8] + (
                t[0][7 : CHUNK + 7] + t[1][8 : CHUNK + 8] + t[2][9 : CHUNK + 9]
            )
            gx[r, pl.ds(at, CHUNK), :] = res.astype(BF16)
            return carry

        lax.fori_loop(0, COLS // CHUNK, chunk, 0)

    def span(part):
        first, width, _ = PARTS[part]
        return slice(first, first + width)

    def swap(part):
        cols = span(part)
        return remote(
            grads.at[1 - core, :, cols], r0.at[:, cols], bsem.at[0, part], bsem.at[1, part], twin
        )

    def swap_end(part):
        cols = span(part)
        swap(part).wait()

        def add(c, carry):
            rows = pl.ds(pl.multiple_of(c * 32, 32), 32)
            a0[rows, cols] = (grads[core, rows, cols].astype(F32) + r0[rows, cols].astype(F32)).astype(BF16)
            return carry

        lax.fori_loop(0, 8, add, 0)

    def stage(k, part, waits):
        first, width, axes = PARTS[part]
        axis = axes[k]
        for d in range(1, 4):
            j = ahead(axis, d)
            if k == 0:
                src = a0.at[pl.ds(pl.multiple_of(j * 64, 64), 64), span(part)]
                dst = r1.at[part, d - 1, :, 0:width]
            elif k == 1:
                src = a1.at[part, pl.ds(pl.multiple_of(j * 16, 16), 16), 0:width]
                dst = r2.at[part, d - 1, :, 0:width]
            else:
                src = ex.at[part, coord[axis], :, 0:width]
                dst = ex.at[part, behind(axis, d) if waits else coord[axis], :, 0:width]
            cp = remote(src, dst, rsem.at[0, k, part, d], rsem.at[1, k, part, d], at_axis(axis, j))
            if waits:
                cp.wait()
            else:
                cp.start()

    def stage_start(k):
        for part in range(3):
            stage(k, part, False)

    def stage_end(k, part):
        first, width, axes = PARTS[part]
        stage(k, part, True)
        m = coord[axes[k]]
        if k == 0:
            t = a0[pl.ds(pl.multiple_of(m * 64, 64), 64), span(part)].astype(F32)
            for d in range(3):
                t = t + r1[part, d, :, 0:width].astype(F32)
            a1[part, :, 0:width] = t.astype(BF16)
        elif k == 1:
            t = a1[part, pl.ds(pl.multiple_of(m * 16, 16), 16), 0:width].astype(F32)
            for d in range(3):
                t = t + r2[part, d, :, 0:width].astype(F32)
            ex[part, coord[axes[2]], :, 0:width] = t.astype(BF16)
        else:
            t = ex[part, 0, :, 0:width].astype(F32)
            for d in range(1, 4):
                t = t + ex[part, d, :, 0:width].astype(F32)
            rows = pl.multiple_of(coord[axes[0]] * 64 + coord[axes[1]] * 16, 16)
            total[core, pl.ds(rows, 16), span(part)] = t.astype(BF16)

    def block(k, part, values):
        if k == 0:
            return total.at[core, pl.ds(pl.multiple_of(values[0] * 64, 64), 64), span(part)]
        return total.at[core, pl.ds(pl.multiple_of(values[0] * 64 + values[1] * 16, 16), 16), span(part)]

    def gather(k, part, waits):
        axes = PARTS[part][2]
        mine = [coord[ax] for ax in axes]
        for d in range(1, 4):
            theirs = list(mine)
            theirs[k] = behind(axes[k], d)
            src = block(k, part, mine)
            dst = block(k, part, theirs) if waits else src
            cp = remote(src, dst, gsem.at[0, k, part, d], gsem.at[1, k, part, d], at_axis(axes[k], ahead(axes[k], d)))
            if waits:
                cp.wait()
            else:
                cp.start()

    def twin_gather(part, waits):
        dst = total.at[(1 - core) if waits else core, :, span(part)]
        cp = remote(total.at[core, :, span(part)], dst, bsem.at[0, 3 + part], bsem.at[1, 3 + part], twin)
        if waits:
            cp.wait()
        else:
            cp.start()

    def small_stage(slots, axis, k, waits):
        m = coord[axis]
        for d in range(1, 4):
            dst = slots.at[behind(axis, d)] if waits else slots.at[m]
            cp = remote(slots.at[m], dst, ssem.at[0, k, d], ssem.at[1, k, d], at_axis(axis, ahead(axis, d)))
            if waits:
                cp.wait()
            else:
                cp.start()

    def small_twin(dst):
        return remote(s4.at[core], s4.at[dst], ssem.at[0, 3, 0], ssem.at[1, 3, 0], twin)

    def widen(r, c):
        xp[r + 1, 8 : COLS + 8, :] = latent[r].astype(F32)
        return c

    cot_row(1)
    lax.fori_loop(0, ROWS, widen, 0)

    def inner_row(i, c):
        norm_row(1 + i)

        @pl.when(i == 0)
        def _():
            cot_row(2)

        return c

    lax.fori_loop(0, 2, inner_row, 0)
    cot_row(0)
    loads[2].wait()
    loads[3].wait()

    def edge_row(i, c):
        norm_row(3 * i)

        @pl.when(i == 0)
        def _():
            cot_row(3)

        return c

    def step(i, c):
        r = jnp.where(i < 2, i + 1, (i - 2) * 3)
        finish(cs, cr, csem, r)
        finish(xs, xr, xsem, r)
        attention_row(
            xr[r].reshape(COLS, D), cr[r].reshape(COLS, D), wqkv, wout, xg, cg, qkv, da, att, dp, gperm, r
        )
        dn[r] = normed_back(dp, wqkv, r)
        send(dn, dr, dsem, r)

        @pl.when(i == 0)
        def _():
            edge_wait(latent.at[0], latent.at[3], halo, hsem)
            xp[0, 8 : COLS + 8, :] = halo[0].astype(F32)
            xp[ROWS + 1, 8 : COLS + 8, :] = halo[1].astype(F32)
            lax.fori_loop(0, 2, edge_row, 0)

        return c

    lax.fori_loop(0, ROWS, step, 0)
    weight_grads(xg, cg, att, dp, grads, 1 - core)
    for part in range(3):
        swap(part).start()
    weight_grads(xg, cg, att, dp, grads, core)
    for part in range(3):
        swap_end(part)
        stage(0, part, False)
    back_row(0)
    hsend[0] = dpad[1, 8 : COLS + 8, :].astype(BF16)
    edge_start((hsend.at[0], hrecv), None, wsem)
    back_row(3)
    hsend[1] = dpad[4, 8 : COLS + 8, :].astype(BF16)
    edge_start(None, (hsend.at[1], hrecv), wsem)
    for part in range(3):
        stage_end(0, part)
        stage(1, part, False)
    back_row(1)
    back_row(2)
    for part in range(3):
        stage_end(1, part)
        stage(2, part, False)
    kernel_rows(0, 4)
    for n in range(9):
        sm[n : n + 1, :] = jnp.sum(ksum[n], axis=0, keepdims=True)
    for n in range(2):
        sm[9 + n : 10 + n, :] = jnp.sum(tsum[n], axis=0, keepdims=True)
    sm[11:12, :] = leadrow[0:1, :]
    sm[12:16, :] = jnp.zeros((4, D), F32)
    s1[z] = sm[...]
    small_stage(s1, "z", 0, False)
    for part in range(3):
        stage_end(2, part)
        gather(1, part, False)
    out_row(1)
    out_row(2)
    small_stage(s1, "z", 0, True)
    s2[y] = s1[0] + s1[1] + s1[2] + s1[3]
    small_stage(s2, "y", 1, False)
    for part in range(3):
        gather(1, part, True)
        gather(0, part, False)
    edge_wait(hsend.at[0], hsend.at[1], hrecv, wsem)
    dpad[0, 8 : COLS + 8, :] = hrecv[0].astype(F32)
    dpad[ROWS + 1, 8 : COLS + 8, :] = hrecv[1].astype(F32)
    out_row(0)
    small_stage(s2, "y", 1, True)
    s3[x] = s2[0] + s2[1] + s2[2] + s2[3]
    small_stage(s3, "x", 2, False)
    out_row(3)
    for part in range(3):
        gather(0, part, True)
        twin_gather(part, False)
    small_stage(s3, "x", 2, True)
    s4[core, 0] = s3[0] + s3[2]
    s4[core, 1] = s3[1] + s3[3]
    small_twin(core).start()
    small_twin(1 - core).wait()
    small[...] = s4[...]
    for part in range(3):
        twin_gather(part, True)


STEPS = 4


def finish_kernel(norm_scale, table_rows, total, small, grad_qkv, grad_out, grad_kernel, grad_table):
    step = pl.program_id(0)
    whole = total[0].astype(F32) * norm_scale
    grad_qkv[...] = whole[:, : 3 * D]
    grad_out[...] = whole[:, 3 * D :]
    for n in range(9):
        row = small[0, n : n + 1, :]
        for m in range(1, 4):
            row = row + small[m, n : n + 1, :]
        grad_kernel[n // 3, n % 3 : n % 3 + 1, :] = row * norm_scale
    grad_table[...] = jnp.zeros(grad_table.shape, F32)
    for m in range(4):
        index = (jnp.max(small[m, 11:12, 0:128]) + 0.5).astype(jnp.int32) - step * table_rows

        @pl.when((index >= 0) & (index < table_rows))
        def _():
            grad_table[index] = grad_table[index] + small[m, 9:11, :] * norm_scale


def vmem(count):
    return [pl.BlockSpec(memory_space=pltpu.VMEM)] * count


def per_device(latent, lead_index, conv_kernel, cond_table, w_qkv, w_out, cotangent):
    leads = cond_table.shape[0]
    norm_scale = 1.0 / math.sqrt(4 * 128 * 256)
    ck = conv_kernel.reshape(9, D)
    mod = lax.dynamic_index_in_dim(cond_table, lead_index[0], 0, keepdims=False)
    leadrow = jnp.broadcast_to(lead_index[0].astype(F32) * (1.0 / 32.0), (8, D))
    shape = jax.ShapeDtypeStruct
    far = pl.BlockSpec(memory_space=pl.ANY)
    near = pl.BlockSpec(memory_space=pltpu.VMEM)
    dma = pltpu.SemaphoreType.DMA
    f32 = lambda *dims: pltpu.VMEM(dims, F32)
    bf16 = lambda *dims: pltpu.VMEM(dims, BF16)
    blocks = (ROWS, PEERS, CHUNK, D)

    grad_x, total, small = pl.pallas_call(
        section_kernel,
        out_shape=[
            shape((ROWS, COLS, D), BF16),
            shape((2, 256, 4 * D), BF16),
            shape((2, 2, 16, D), F32),
        ],
        in_specs=[far, far, near, near, far, far, near],
        out_specs=[near, near, near],
        scratch_shapes=[
            bf16(ROWS, COLS, D),
            bf16(ROWS, COLS, D),
            bf16(D, 3 * D),
            bf16(D, D),
            bf16(2, COLS, D),
            f32(ROWS + 2, COLS + 16, D),
            f32(ROWS + 2, COLS + 16, D),
            f32(ROWS, COLS, D),
            f32(ROWS, COLS, 128),
            bf16(COLS, D),
            bf16(COLS, COLS),
            bf16(COLS, COLS),
            bf16(COLS, COLS),
            bf16(*blocks),
            bf16(*blocks),
            bf16(*blocks),
            bf16(*blocks),
            bf16(ROWS * COLS, D),
            bf16(ROWS * COLS, D),
            bf16(COLS, 3 * D),
            bf16(COLS, D),
            bf16(ROWS * COLS, D),
            bf16(ROWS * COLS, 3 * D),
            bf16(*blocks),
            bf16(*blocks),
            f32(COLS, D),
            bf16(2, COLS, D),
            bf16(2, COLS, D),
            bf16(2, 256, 4 * D),
            bf16(256, 4 * D),
            bf16(256, 4 * D),
            bf16(3, 3, 64, 768),
            bf16(3, 64, 768),
            bf16(3, 3, 16, 768),
            bf16(3, 4, 16, 768),
            f32(9, 8, D),
            f32(2, 8, D),
            f32(16, D),
            f32(4, 16, D),
            f32(4, 16, D),
            f32(4, 16, D),
            f32(2, 2, 16, D),
            dma((4,)),
            dma((4,)),
            dma((2, ROWS, PEERS)),
            dma((2, ROWS, PEERS)),
            dma((2, ROWS, PEERS)),
            dma((2, 6)),
            dma((4,)),
            dma((2, 3, 3, 4)),
            dma((2, 2, 3, 4)),
            dma((2, 4, 4)),
        ],
        compiler_params=pltpu.CompilerParams(
            collective_id=1, has_side_effects=True, vmem_limit_bytes=VMEM_LIMIT
        ),
        name="section",
    )(latent[0], cotangent[0], ck, mod, w_qkv, w_out, leadrow)

    table_rows = -(-leads // STEPS)
    grad_qkv, grad_out, grad_kernel, grad_table = pl.pallas_call(
        functools.partial(finish_kernel, norm_scale, table_rows),
        grid=(STEPS,),
        out_shape=[
            shape((D, 3 * D), F32),
            shape((D, D), F32),
            shape((3, 3, D), F32),
            shape((leads, 2, D), F32),
        ],
        in_specs=[
            pl.BlockSpec((1, 512 // STEPS, 4 * D), lambda i: (i // 2, i % 2, 0)),
            pl.BlockSpec((4, 16, D), lambda i: (0, 0, 0)),
        ],
        out_specs=[
            pl.BlockSpec((512 // STEPS, 3 * D), lambda i: (i, 0)),
            pl.BlockSpec((512 // STEPS, D), lambda i: (i, 0)),
            pl.BlockSpec((3, 3, D), lambda i: (0, 0, 0)),
            pl.BlockSpec((table_rows, 2, D), lambda i: (i, 0, 0)),
        ],
        compiler_params=pltpu.CompilerParams(vmem_limit_bytes=VMEM_LIMIT),
        name="finish",
    )(total, small.reshape(4, 16, D))
    return (grad_x[None], grad_qkv, grad_out, grad_kernel, grad_table)


def solution(mesh):
    in_specs = (
        P("lead", "space", None, None),
        P("lead"),
        P(),
        P(),
        P(),
        P(),
        P("lead", "space", None, None),
    )
    out_specs = (P("lead", "space", None, None), P(), P(), P(), P())
    return jax.shard_map(
        per_device, mesh=mesh, in_specs=in_specs, out_specs=out_specs, check_vma=False
    )
```

profile of v0, /device:TPU:1, one launch (start us, length us, event | category | flops | bytes accessed | tf_op | source)
XLA Modules:
  0.0 104.0 jit_solution(11370588036874261934)
XLA Ops:
  0.6 0.0 copy-start
  1.4 1.0 copy-done
  2.5 0.8 reshape.16.ck
  3.2 0.0 copy-start.1
  3.3 1.0 copy-done.1
  4.3 92.8 %section.1 = (bf16[4,256,512]{2,1,0:T(8,128)(2,1)S(1)}, bf16[2,256,2048]{2,1,0:T(8,128)(2,1)}, f32[2,2,16,512]{3,2,1,0:T(8,128)S(1)}) custom-call(bf16[4,256,512]{2,1,0:T(8,128)(2,1)} %bitcast.13, bf16[4,256,512]{2,1,0:T(8,128)(2,1)} %bitcast.14, f32[9,512]{1,0:T(8,128)S(1)} %reshape.16.ck, f32[2,512]{1,0:T(2,128)S(1)} %dynamic-slice_bitcast_fusion.mod, ...), custom_call_target="tpu_custom_call" | custom-call | tf_op jit(solution)/shard_map/section/pallas_call | solution.py:593
  97.1 5.9 %finish.1 = (f32[512,1536]{1,0:T(8,128)}, f32[512,512]{1,0:T(8,128)}, f32[3,3,512]{2,1,0:T(4,128)}, f32[721,2,512]{2,1,0:T(2,128)}) custom-call(bf16[2,256,2048]{2,1,0:T(8,128)(2,1)} %get-tuple-element.13.total, f32[4,16,512]{2,1,0:T(8,128)S(1)} %bitcast.12), custom_call_target="tpu_custom_call" | custom-call | tf_op jit(solution)/shard_map/finish/pallas_call | solution.py:663
  103.0 1.0 copy.14
  (2 shorter events, 0.0 us)
Async XLA Ops:
  0.6 1.9 %copy-start = (f32[721,2,512]{2,1,0:T(2,128)S(1)}, f32[721,2,512]{2,1,0:T(2,128)}, u32[]{:S(2)}) copy-start(f32[721,2,512]{2,1,0:T(2,128)} %param.10) | copy-start | bytes 8859652
  3.2 1.0 %copy-start.1 = (bf16[512,512]{1,0:T(8,128)(2,1)S(1)}, bf16[512,512]{1,0:T(8,128)(2,1)}, u32[]{:S(2)}) copy-start(bf16[512,512]{1,0:T(8,128)(2,1)} %wout_any.1) | copy-start | bytes 1572868
where the time goes:
time: 104 us
  Pallas kernels  98.7 us (95%)
  local copies, waits for them, and re-layouts  3.81 us (4%)
  between operations  1.46 us (1%)
    pallas_call x1, Pallas kernels, per_device(): pl.pallas_call(section_kernel, out_shape=[shape((ROWS, COLS, D), BF16), s...  92.8 us
    pallas_call x1, Pallas kernels, per_device(): pl.pallas_call(functools.partial(finish_kernel, norm_scale, table_rows),...  5.93 us
    unnamed x5, local copies, waits for them, and re-layouts  3.05 us

commit v1 on v0

--- a/solution.py
+++ b/solution.py
@@ -19,7 +19,7 @@
 MESH = pl.DeviceIdType.MESH
 F32 = jnp.float32
 BF16 = jnp.bfloat16
-VMEM_LIMIT = 52 * 1024 * 1024
+VMEM_LIMIT = 61 * 1024 * 1024
 
 
 def remote(src, dst, send, recv, device):
@@ -112,23 +112,32 @@
     return jnp.concatenate(blocks, axis=0).astype(BF16).reshape(PEERS, CHUNK, D)
 
 
-def weight_grads(xg, cg, att, dp, grads, h):
-    half = pl.ds(pl.multiple_of(h * 256, 256), 256)
-    for n in range(3):
-        grads[h, :, n * D : (n + 1) * D] = dot(xg[:, half], dp[:, n * D : (n + 1) * D], 0, 0).astype(BF16)
-    grads[h, :, 3 * D :] = dot(att[:, half], cg[...], 0, 0).astype(BF16)
+def grads_of(xg, cg, att, dp, here, half, n):
+    if n < 3:
+        return dot(xg[here, half], dp[here, n * D : (n + 1) * D], 0, 0)
+    return dot(att[here, half], cg[here, :], 0, 0)
+
+
+def add_grads(xg, cg, att, dp, acc, i):
+    here = pl.ds(pl.multiple_of(i * COLS, COLS), COLS)
+    for h in range(2):
+        for n in range(4):
+            half = slice(h * 256, h * 256 + 256)
+            acc[h, :, n * D : (n + 1) * D] += grads_of(xg, cg, att, dp, here, half, n)
 
 
 PARTS = ((0, 640, "xyz"), (640, 640, "yzx"), (1280, 768, "zxy"))
+NP = len(PARTS)
+WIDE = 768
 
 
 def section_kernel(
-    latent_any, cot_any, ck, mod, wqkv_any, wout_any, leadrow,
-    gx, total, small,
-    latent, cot, wqkv, wout, halo, xp, dpad, nf, inv, nrm, fperm, gperm, bperm,
+    latent_any, cot_any, ck, lead_index, cond_any, wqkv_any, wout_any,
+    gx_any, total_any, small,
+    gx, total, latent, cot, wqkv, wout, cond, mod, halo, xp, dpad, nf, inv, nrm, fperm, gperm, bperm,
     xs, cs, xr, cr, xg, cg, qkv, da, att, dp, dn, dr, dnf, hsend, hrecv,
-    grads, r0, a0, r1, a1, r2, ex, ksum, tsum, sm, s1, s2, s3, s4,
-    lsem, hsem, xsem, csem, dsem, bsem, wsem, rsem, gsem, ssem,
+    acc, grads, r0, a0, r1, a1, r2, ex, ksum, tsum, sm, s1, s2, s3, s4,
+    lsem, hsem, xsem, csem, dsem, bsem, wsem, rsem, gsem, ssem, osem,
 ):
     lead = lax.axis_index("lead")
     space = lax.axis_index("space")
@@ -157,7 +166,16 @@
     loads = [
         pltpu.make_async_copy(src, dst, lsem.at[n])
         for n, (src, dst) in enumerate(
-            ((latent_any, latent), (cot_any, cot), (wqkv_any, wqkv), (wout_any, wout))
+            (
+                (cot_any.at[1], cot.at[1]),
+                (latent_any.at[0:2], latent.at[0:2]),
+                (latent_any.at[2:4], latent.at[2:4]),
+                (cond_any, cond),
+                (cot_any.at[2:4], cot.at[2:4]),
+                (cot_any.at[0], cot.at[0]),
+                (wqkv_any, wqkv),
+                (wout_any, wout),
+            )
         )
     ]
     for load in loads:
@@ -197,41 +215,35 @@
         greet((lead, space + 1))
 
     fperm[...] = send_order()
-    gperm[...] = group_order()
-    bperm[...] = field_order()
-    xp[:, 0:8, :] = jnp.zeros((ROWS + 2, 8, D), F32)
-    xp[:, COLS + 8 : COLS + 16, :] = jnp.zeros((ROWS + 2, 8, D), F32)
-    dpad[:, 0:8, :] = jnp.zeros((ROWS + 2, 8, D), F32)
-    dpad[:, COLS + 8 : COLS + 16, :] = jnp.zeros((ROWS + 2, 8, D), F32)
-    ksum[...] = jnp.zeros((9, 8, D), F32)
-    tsum[...] = jnp.zeros((2, 8, D), F32)
-    loads[0].wait()
-    loads[1].wait()
     pl.semaphore_wait(barrier, 17 + jnp.where(has_low, 1, 0) + jnp.where(has_high, 1, 0))
 
-    def edge_start(low, high, sem):
-        @pl.when(has_low)
+    def edge(src, dst, piece, sem, up):
+        cells = slice(piece * 128, piece * 128 + 128)
+        n = 2 * piece + (0 if up else 4)
+        device = (lead, space - 1) if up else (lead, space + 1)
+        return remote(src.at[cells], dst.at[1 if up else 0, cells], sem.at[n], sem.at[n + 1], device)
+
+    def edge_start(src, dst, piece, sem, up):
+        @pl.when(has_low if up else has_high)
         def _():
-            if low is not None:
-                remote(low[0], low[1].at[1], sem.at[0], sem.at[2], (lead, space - 1)).start()
-
-        @pl.when(has_high)
-        def _():
-            if high is not None:
-                remote(high[0], high[1].at[0], sem.at[1], sem.at[3], (lead, space + 1)).start()
+            edge(src, dst, piece, sem, up).start()
 
     def edge_wait(first, last, dst, sem):
-        @pl.when(has_low)
-        def _():
-            remote(first, dst.at[1], sem.at[0], sem.at[2], (lead, space - 1)).wait_send()
-            remote(last, dst.at[0], sem.at[1], sem.at[3], (lead, space - 1)).wait_recv()
-
-        @pl.when(has_high)
-        def _():
-            remote(last, dst.at[0], sem.at[1], sem.at[3], (lead, space + 1)).wait_send()
-            remote(first, dst.at[1], sem.at[0], sem.at[2], (lead, space + 1)).wait_recv()
-
-    edge_start((latent.at[0], halo), (latent.at[3], halo), hsem)
+        for piece in range(2):
+
+            @pl.when(has_low)
+            def _():
+                edge(first, dst, piece, sem, True).wait_send()
+                edge(last, dst, piece, sem, False).wait_recv()
+
+            @pl.when(has_high)
+            def _():
+                edge(last, dst, piece, sem, False).wait_send()
+                edge(first, dst, piece, sem, True).wait_recv()
+
+    for piece in range(2):
+        edge_start(latent_any.at[0], halo, piece, hsem, True)
+        edge_start(latent_any.at[3], halo, piece, hsem, False)
 
     def send(bufs, out, sem, r):
         def one(d, c):
@@ -260,7 +272,7 @@
         def chunk(c, carry):
             at = pl.multiple_of(c * CHUNK, CHUNK)
             w = [xp[r + m, pl.ds(at, CHUNK + 16), :] for m in range(3)]
-            k = [ck[m : m + 1, :] for m in range(9)]
+            k = [ck[m // 3, m % 3 : m % 3 + 1, :] for m in range(9)]
             t = [k[j] * w[0] + k[3 + j] * w[1] + k[6 + j] * w[2] for j in range(3)]
             res = w[1][8 : CHUNK + 8] + (
                 t[0][7 : CHUNK + 7] + t[1][8 : CHUNK + 8] + t[2][9 : CHUNK + 9]
@@ -275,7 +287,6 @@
 
         lax.fori_loop(0, COLS // CHUNK, chunk, 0)
         xs[r] = dot(fperm[...], nrm[...], 1, 0).astype(BF16).reshape(PEERS, CHUNK, D)
-        send(xs, xr, xsem, r)
 
     def fold(t):
         total = t[0:8]
@@ -322,7 +333,7 @@
         def chunk(c, carry):
             at = pl.multiple_of(c * CHUNK, CHUNK)
             w = [dpad[r + m, pl.ds(at, CHUNK + 16), :] for m in range(3)]
-            k = [ck[m : m + 1, :] for m in range(9)]
+            k = [ck[m // 3, m % 3 : m % 3 + 1, :] for m in range(9)]
             t = [k[8 - j] * w[0] + k[5 - j] * w[1] + k[2 - j] * w[2] for j in range(3)]
             res = w[1][8 : CHUNK + 8] + (
                 t[0][7 : CHUNK + 7] + t[1][8 : CHUNK + 8] + t[2][9 : CHUNK + 9]
@@ -331,6 +342,7 @@
             return carry
 
         lax.fori_loop(0, COLS // CHUNK, chunk, 0)
+        keep_row(r).start()
 
     def span(part):
         first, width, _ = PARTS[part]
@@ -339,7 +351,7 @@
     def swap(part):
         cols = span(part)
         return remote(
-            grads.at[1 - core, :, cols], r0.at[:, cols], bsem.at[0, part], bsem.at[1, part], twin
+            grads.at[:, cols], r0.at[:, cols], bsem.at[0, part], bsem.at[1, part], twin
         )
 
     def swap_end(part):
@@ -348,7 +360,7 @@
 
         def add(c, carry):
             rows = pl.ds(pl.multiple_of(c * 32, 32), 32)
-            a0[rows, cols] = (grads[core, rows, cols].astype(F32) + r0[rows, cols].astype(F32)).astype(BF16)
+            a0[rows, cols] = (acc[core, rows, cols] + r0[rows, cols].astype(F32)).astype(BF16)
             return carry
 
         lax.fori_loop(0, 8, add, 0)
@@ -374,7 +386,7 @@
                 cp.start()
 
     def stage_start(k):
-        for part in range(3):
+        for part in range(NP):
             stage(k, part, False)
 
     def stage_end(k, part):
@@ -396,12 +408,12 @@
             for d in range(1, 4):
                 t = t + ex[part, d, :, 0:width].astype(F32)
             rows = pl.multiple_of(coord[axes[0]] * 64 + coord[axes[1]] * 16, 16)
-            total[core, pl.ds(rows, 16), span(part)] = t.astype(BF16)
+            total[pl.ds(rows, 16), span(part)] = t.astype(BF16)
 
     def block(k, part, values):
         if k == 0:
-            return total.at[core, pl.ds(pl.multiple_of(values[0] * 64, 64), 64), span(part)]
-        return total.at[core, pl.ds(pl.multiple_of(values[0] * 64 + values[1] * 16, 16), 16), span(part)]
+            return total.at[pl.ds(pl.multiple_of(values[0] * 64, 64), 64), span(part)]
+        return total.at[pl.ds(pl.multiple_of(values[0] * 64 + values[1] * 16, 16), 16), span(part)]
 
     def gather(k, part, waits):
         axes = PARTS[part][2]
@@ -417,13 +429,22 @@
             else:
                 cp.start()
 
+    def keep(part):
+        return pltpu.make_async_copy(
+            total.at[:, span(part)], total_any.at[core, :, span(part)], osem.at[part]
+        )
+
     def twin_gather(part, waits):
-        dst = total.at[(1 - core) if waits else core, :, span(part)]
-        cp = remote(total.at[core, :, span(part)], dst, bsem.at[0, 3 + part], bsem.at[1, 3 + part], twin)
+        keep(part).wait() if waits else keep(part).start()
+        dst = total_any.at[(1 - core) if waits else core, :, span(part)]
+        cp = remote(total.at[:, span(part)], dst, bsem.at[0, NP + part], bsem.at[1, NP + part], twin)
         if waits:
             cp.wait()
         else:
             cp.start()
+
+    def keep_row(r):
+        return pltpu.make_async_copy(gx.at[r], gx_any.at[r], osem.at[NP + r])
 
     def small_stage(slots, axis, k, waits):
         m = coord[axis]
@@ -442,11 +463,20 @@
         xp[r + 1, 8 : COLS + 8, :] = latent[r].astype(F32)
         return c
 
+    loads[0].wait()
     cot_row(1)
+    xp[:, 0:8, :] = jnp.zeros((ROWS + 2, 8, D), F32)
+    xp[:, COLS + 8 : COLS + 16, :] = jnp.zeros((ROWS + 2, 8, D), F32)
+    loads[1].wait()
+    loads[2].wait()
     lax.fori_loop(0, ROWS, widen, 0)
+    loads[3].wait()
+    mod[...] = cond[lead_index[0]]
+    loads[4].wait()
 
     def inner_row(i, c):
         norm_row(1 + i)
+        send(xs, xr, xsem, 1 + i)
 
         @pl.when(i == 0)
         def _():
@@ -455,17 +485,22 @@
         return c
 
     lax.fori_loop(0, 2, inner_row, 0)
+    loads[5].wait()
     cot_row(0)
-    loads[2].wait()
-    loads[3].wait()
+    cot_row(3)
+    gperm[...] = group_order()
+    bperm[...] = field_order()
+    dpad[:, 0:8, :] = jnp.zeros((ROWS + 2, 8, D), F32)
+    dpad[:, COLS + 8 : COLS + 16, :] = jnp.zeros((ROWS + 2, 8, D), F32)
+    ksum[...] = jnp.zeros((9, 8, D), F32)
+    tsum[...] = jnp.zeros((2, 8, D), F32)
+    acc[...] = jnp.zeros(acc.shape, F32)
+    loads[6].wait()
+    loads[7].wait()
 
     def edge_row(i, c):
         norm_row(3 * i)
-
-        @pl.when(i == 0)
-        def _():
-            cot_row(3)
-
+        send(xs, xr, xsem, 3 * i)
         return c
 
     def step(i, c):
@@ -473,84 +508,99 @@
         finish(cs, cr, csem, r)
         finish(xs, xr, xsem, r)
         attention_row(
-            xr[r].reshape(COLS, D), cr[r].reshape(COLS, D), wqkv, wout, xg, cg, qkv, da, att, dp, gperm, r
+            xr[r].reshape(COLS, D), cr[r].reshape(COLS, D), wqkv, wout, xg, cg, qkv, da, att, dp, gperm, i
         )
-        dn[r] = normed_back(dp, wqkv, r)
-        send(dn, dr, dsem, r)
 
         @pl.when(i == 0)
         def _():
-            edge_wait(latent.at[0], latent.at[3], halo, hsem)
+            edge_wait(latent_any.at[0], latent_any.at[3], halo, hsem)
             xp[0, 8 : COLS + 8, :] = halo[0].astype(F32)
             xp[ROWS + 1, 8 : COLS + 8, :] = halo[1].astype(F32)
             lax.fori_loop(0, 2, edge_row, 0)
 
+        dn[r] = normed_back(dp, wqkv, i)
+        send(dn, dr, dsem, r)
+
+        @pl.when(i < 2)
+        def _():
+            add_grads(xg, cg, att, dp, acc, i)
+
         return c
 
     lax.fori_loop(0, ROWS, step, 0)
-    weight_grads(xg, cg, att, dp, grads, 1 - core)
-    for part in range(3):
+    late = slice(2 * COLS, 4 * COLS)
+    theirs = pl.ds(pl.multiple_of((1 - core) * 256, 256), 256)
+    ours = pl.ds(pl.multiple_of(core * 256, 256), 256)
+    for n in range(4):
+        cols = slice(n * D, (n + 1) * D)
+        grads[:, cols] = (acc[1 - core, :, cols] + grads_of(xg, cg, att, dp, late, theirs, n)).astype(BF16)
+    for part in range(NP):
         swap(part).start()
-    weight_grads(xg, cg, att, dp, grads, core)
-    for part in range(3):
+    for n in range(4):
+        acc[core, :, n * D : (n + 1) * D] += grads_of(xg, cg, att, dp, late, ours, n)
+    back_row(0)
+    hsend[0] = dpad[1, 8 : COLS + 8, :].astype(BF16)
+    for piece in range(2):
+        edge_start(hsend.at[0], hrecv, piece, wsem, True)
+    for part in range(NP):
         swap_end(part)
         stage(0, part, False)
-    back_row(0)
-    hsend[0] = dpad[1, 8 : COLS + 8, :].astype(BF16)
-    edge_start((hsend.at[0], hrecv), None, wsem)
+    back_row(1)
+    back_row(2)
     back_row(3)
     hsend[1] = dpad[4, 8 : COLS + 8, :].astype(BF16)
-    edge_start(None, (hsend.at[1], hrecv), wsem)
-    for part in range(3):
+    for piece in range(2):
+        edge_start(hsend.at[1], hrecv, piece, wsem, False)
+    for part in range(NP):
         stage_end(0, part)
         stage(1, part, False)
-    back_row(1)
-    back_row(2)
-    for part in range(3):
-        stage_end(1, part)
-        stage(2, part, False)
     kernel_rows(0, 4)
     for n in range(9):
         sm[n : n + 1, :] = jnp.sum(ksum[n], axis=0, keepdims=True)
     for n in range(2):
         sm[9 + n : 10 + n, :] = jnp.sum(tsum[n], axis=0, keepdims=True)
-    sm[11:12, :] = leadrow[0:1, :]
+    sm[11:12, :] = jnp.full((1, D), lead_index[0].astype(F32) * (1.0 / 32.0))
     sm[12:16, :] = jnp.zeros((4, D), F32)
     s1[z] = sm[...]
     small_stage(s1, "z", 0, False)
-    for part in range(3):
-        stage_end(2, part)
-        gather(1, part, False)
+    for part in range(NP):
+        stage_end(1, part)
+        stage(2, part, False)
     out_row(1)
     out_row(2)
     small_stage(s1, "z", 0, True)
     s2[y] = s1[0] + s1[1] + s1[2] + s1[3]
     small_stage(s2, "y", 1, False)
-    for part in range(3):
+    for part in range(NP):
+        stage_end(2, part)
+        gather(1, part, False)
+    small_stage(s2, "y", 1, True)
+    s3[x] = s2[0] + s2[1] + s2[2] + s2[3]
+    small_stage(s3, "x", 2, False)
+    for part in range(NP):
         gather(1, part, True)
         gather(0, part, False)
     edge_wait(hsend.at[0], hsend.at[1], hrecv, wsem)
     dpad[0, 8 : COLS + 8, :] = hrecv[0].astype(F32)
     dpad[ROWS + 1, 8 : COLS + 8, :] = hrecv[1].astype(F32)
     out_row(0)
-    small_stage(s2, "y", 1, True)
-    s3[x] = s2[0] + s2[1] + s2[2] + s2[3]
-    small_stage(s3, "x", 2, False)
     out_row(3)
-    for part in range(3):
-        gather(0, part, True)
-        twin_gather(part, False)
     small_stage(s3, "x", 2, True)
     s4[core, 0] = s3[0] + s3[2]
     s4[core, 1] = s3[1] + s3[3]
     small_twin(core).start()
+    for part in range(NP):
+        gather(0, part, True)
+        twin_gather(part, False)
     small_twin(1 - core).wait()
     small[...] = s4[...]
-    for part in range(3):
+    for r in range(ROWS):
+        keep_row(r).wait()
+    for part in range(NP):
         twin_gather(part, True)
 
 
-STEPS = 4
+STEPS = 2
 
 
 def finish_kernel(norm_scale, table_rows, total, small, grad_qkv, grad_out, grad_kernel, grad_table):
@@ -579,9 +629,6 @@
 def per_device(latent, lead_index, conv_kernel, cond_table, w_qkv, w_out, cotangent):
     leads = cond_table.shape[0]
     norm_scale = 1.0 / math.sqrt(4 * 128 * 256)
-    ck = conv_kernel.reshape(9, D)
-    mod = lax.dynamic_index_in_dim(cond_table, lead_index[0], 0, keepdims=False)
-    leadrow = jnp.broadcast_to(lead_index[0].astype(F32) * (1.0 / 32.0), (8, D))
     shape = jax.ShapeDtypeStruct
     far = pl.BlockSpec(memory_space=pl.ANY)
     near = pl.BlockSpec(memory_space=pltpu.VMEM)
@@ -597,13 +644,17 @@
             shape((2, 256, 4 * D), BF16),
             shape((2, 2, 16, D), F32),
         ],
-        in_specs=[far, far, near, near, far, far, near],
-        out_specs=[near, near, near],
+        in_specs=[far, far, near, pl.BlockSpec(memory_space=pltpu.SMEM), far, far, far],
+        out_specs=[far, far, near],
         scratch_shapes=[
+            bf16(ROWS, COLS, D),
+            bf16(256, 4 * D),
             bf16(ROWS, COLS, D),
             bf16(ROWS, COLS, D),
             bf16(D, 3 * D),
             bf16(D, D),
+            f32(leads, 2, D),
+            f32(2, D),
             bf16(2, COLS, D),
             f32(ROWS + 2, COLS + 16, D),
             f32(ROWS + 2, COLS + 16, D),
@@ -628,13 +679,14 @@
             f32(COLS, D),
             bf16(2, COLS, D),
             bf16(2, COLS, D),
-            bf16(2, 256, 4 * D),
+            f32(2, 256, 4 * D),
             bf16(256, 4 * D),
             bf16(256, 4 * D),
-            bf16(3, 3, 64, 768),
-            bf16(3, 64, 768),
-            bf16(3, 3, 16, 768),
-            bf16(3, 4, 16, 768),
+            bf16(256, 4 * D),
+            bf16(NP, 3, 64, WIDE),
+            bf16(NP, 64, WIDE),
+            bf16(NP, 3, 16, WIDE),
+            bf16(NP, 4, 16, WIDE),
             f32(9, 8, D),
             f32(2, 8, D),
             f32(16, D),
@@ -642,22 +694,23 @@
             f32(4, 16, D),
             f32(4, 16, D),
             f32(2, 2, 16, D),
-            dma((4,)),
-            dma((4,)),
+            dma((8,)),
+            dma((8,)),
             dma((2, ROWS, PEERS)),
             dma((2, ROWS, PEERS)),
             dma((2, ROWS, PEERS)),
-            dma((2, 6)),
-            dma((4,)),
-            dma((2, 3, 3, 4)),
-            dma((2, 2, 3, 4)),
+            dma((2, 2 * NP)),
+            dma((8,)),
+            dma((2, 3, NP, 4)),
+            dma((2, 2, NP, 4)),
             dma((2, 4, 4)),
+            dma((NP + ROWS,)),
         ],
         compiler_params=pltpu.CompilerParams(
             collective_id=1, has_side_effects=True, vmem_limit_bytes=VMEM_LIMIT
         ),
         name="section",
-    )(latent[0], cotangent[0], ck, mod, w_qkv, w_out, leadrow)
+    )(latent[0], cotangent[0], conv_kernel, lead_index, cond_table, w_qkv, w_out)
 
     table_rows = -(-leads // STEPS)
     grad_qkv, grad_out, grad_kernel, grad_table = pl.pallas_call(
@@ -670,7 +723,7 @@
             shape((leads, 2, D), F32),
         ],
         in_specs=[
-            pl.BlockSpec((1, 512 // STEPS, 4 * D), lambda i: (i // 2, i % 2, 0)),
+            pl.BlockSpec((1, 512 // STEPS, 4 * D), lambda i: (i, 0, 0)),
             pl.BlockSpec((4, 16, D), lambda i: (0, 0, 0)),
         ],
         out_specs=[

time: 104 us -> 98.5 us (0.947)
  local copies, waits for them, and re-layouts: 3.81 us -> 0.97 us
  Pallas kernels: 98.7 us -> 96.1 us
    unnamed x5 -> x3, local copies, waits for them, and re-layouts: 3.05 us -> 0.97 us
    pallas_call x1, Pallas kernels: 92.8 us -> 91.1 us  [per_device(): pl.pallas_call(section_kernel, out_shape=[shape((ROWS, COLS, D), BF16), s...]
where the time goes in v1:
time: 98.5 us; the launch traced here: 98.3 us
  Pallas kernels  96.1 us (98%)
  between operations  1.3 us (1%)
    pallas_call x1, Pallas kernels, per_device(): pl.pallas_call(section_kernel, out_shape=[shape((ROWS, COLS, D), BF16), s...  91.1 us
    pallas_call x1, Pallas kernels, per_device(): pl.pallas_call(functools.partial(finish_kernel, norm_scale, table_rows),...  4.99 us

profile of v1, /device:TPU:1, one launch (start us, length us, event | category | flops | bytes accessed | tf_op | source)
XLA Modules:
  0.0 98.3 jit_solution(8229676936606173499)
XLA Ops:
  1.3 91.1 %section.1 = (bf16[4,256,512]{2,1,0:T(8,128)(2,1)}, bf16[2,256,2048]{2,1,0:T(8,128)(2,1)}, f32[2,2,16,512]{3,2,1,0:T(8,128)}) custom-call(bf16[4,256,512]{2,1,0:T(8,128)(2,1)} %bitcast.5, bf16[4,256,512]{2,1,0:T(8,128)(2,1)} %bitcast.6, f32[3,3,512]{2,1,0:T(4,128)} %ck.1, s32[1]{0:T(128)S(6)} %copy.13.lead_index, f32[721,2,512]{2,1,0:T(2,128)} %cond_any.1, ...), custom_call_target="tpu_custom_call" | custom-call | tf_op jit(solution)/shard_map/section/pallas_call | solution.py:640
  92.4 0.0 copy-start
  92.4 5.0 %finish.1 = (f32[512,1536]{1,0:T(8,128)}, f32[512,512]{1,0:T(8,128)}, f32[3,3,512]{2,1,0:T(4,128)}, f32[721,2,512]{2,1,0:T(2,128)}) custom-call(bf16[2,256,2048]{2,1,0:T(8,128)(2,1)} %get-tuple-element.13.total, f32[4,16,512]{2,1,0:T(8,128)} %bitcast.7), custom_call_target="tpu_custom_call" | custom-call | tf_op jit(solution)/shard_map/finish/pallas_call | solution.py:716
  97.4 0.0 copy-done
  97.4 1.0 copy.14
Async XLA Ops:
  92.4 5.0 %copy-start = (bf16[4,256,512]{2,1,0:T(8,128)(2,1)S(1)}, bf16[4,256,512]{2,1,0:T(8,128)(2,1)}, u32[]{:S(2)}) copy-start(bf16[4,256,512]{2,1,0:T(8,128)(2,1)} %get-tuple-element.12) | copy-start | bytes 3145732

commit v2 on v1

--- a/solution.py
+++ b/solution.py
@@ -505,6 +505,7 @@
 
     def step(i, c):
         r = jnp.where(i < 2, i + 1, (i - 2) * 3)
+
         finish(cs, cr, csem, r)
         finish(xs, xr, xsem, r)
         attention_row(
@@ -540,21 +541,18 @@
         acc[core, :, n * D : (n + 1) * D] += grads_of(xg, cg, att, dp, late, ours, n)
     back_row(0)
     hsend[0] = dpad[1, 8 : COLS + 8, :].astype(BF16)
-    for piece in range(2):
-        edge_start(hsend.at[0], hrecv, piece, wsem, True)
     for part in range(NP):
         swap_end(part)
         stage(0, part, False)
     back_row(1)
     back_row(2)
-    back_row(3)
-    hsend[1] = dpad[4, 8 : COLS + 8, :].astype(BF16)
-    for piece in range(2):
-        edge_start(hsend.at[1], hrecv, piece, wsem, False)
+    kernel_rows(0, 3)
     for part in range(NP):
         stage_end(0, part)
         stage(1, part, False)
-    kernel_rows(0, 4)
+    back_row(3)
+    hsend[1] = dpad[4, 8 : COLS + 8, :].astype(BF16)
+    kernel_rows(3, 4)
     for n in range(9):
         sm[n : n + 1, :] = jnp.sum(ksum[n], axis=0, keepdims=True)
     for n in range(2):
@@ -566,6 +564,8 @@
     for part in range(NP):
         stage_end(1, part)
         stage(2, part, False)
+    for piece in range(2):
+        edge_start(hsend.at[0], hrecv, piece, wsem, True)
     out_row(1)
     out_row(2)
     small_stage(s1, "z", 0, True)
@@ -574,6 +574,8 @@
     for part in range(NP):
         stage_end(2, part)
         gather(1, part, False)
+    for piece in range(2):
+        edge_start(hsend.at[1], hrecv, piece, wsem, False)
     small_stage(s2, "y", 1, True)
     s3[x] = s2[0] + s2[1] + s2[2] + s2[3]
     small_stage(s3, "x", 2, False)
@@ -603,8 +605,11 @@
 STEPS = 2
 
 
-def finish_kernel(norm_scale, table_rows, total, small, grad_qkv, grad_out, grad_kernel, grad_table):
+def finish_kernel(
+    norm_scale, table_rows, total, small, gx, grad_qkv, grad_out, grad_kernel, grad_table, grad_x
+):
     step = pl.program_id(0)
+    grad_x[...] = gx[...]
     whole = total[0].astype(F32) * norm_scale
     grad_qkv[...] = whole[:, : 3 * D]
     grad_out[...] = whole[:, 3 * D :]
@@ -713,7 +718,7 @@
     )(latent[0], cotangent[0], conv_kernel, lead_index, cond_table, w_qkv, w_out)
 
     table_rows = -(-leads // STEPS)
-    grad_qkv, grad_out, grad_kernel, grad_table = pl.pallas_call(
+    grad_qkv, grad_out, grad_kernel, grad_table, grad_x = pl.pallas_call(
         functools.partial(finish_kernel, norm_scale, table_rows),
         grid=(STEPS,),
         out_shape=[
@@ -721,20 +726,23 @@
             shape((D, D), F32),
             shape((3, 3, D), F32),
             shape((leads, 2, D), F32),
+            shape((ROWS, COLS, D), BF16),
         ],
         in_specs=[
             pl.BlockSpec((1, 512 // STEPS, 4 * D), lambda i: (i, 0, 0)),
             pl.BlockSpec((4, 16, D), lambda i: (0, 0, 0)),
+            pl.BlockSpec((ROWS // STEPS, COLS, D), lambda i: (i, 0, 0)),
         ],
         out_specs=[
             pl.BlockSpec((512 // STEPS, 3 * D), lambda i: (i, 0)),
             pl.BlockSpec((512 // STEPS, D), lambda i: (i, 0)),
             pl.BlockSpec((3, 3, D), lambda i: (0, 0, 0)),
             pl.BlockSpec((table_rows, 2, D), lambda i: (i, 0, 0)),
+            pl.BlockSpec((ROWS // STEPS, COLS, D), lambda i: (i, 0, 0)),
         ],
         compiler_params=pltpu.CompilerParams(vmem_limit_bytes=VMEM_LIMIT),
         name="finish",
-    )(total, small.reshape(4, 16, D))
+    )(total, small.reshape(4, 16, D), grad_x)
     return (grad_x[None], grad_qkv, grad_out, grad_kernel, grad_table)
 
 

time: 98.5 us -> 95.1 us (0.965)
  Pallas kernels: 96.1 us -> 93.6 us
    pallas_call x1, Pallas kernels: 91.1 us -> 88.2 us  [per_device(): pl.pallas_call(section_kernel, out_shape=[shape((ROWS, COLS, D), BF16), s...]
where the time goes in v2:
time: 95.1 us; the launch traced here: 94.9 us
  Pallas kernels  93.6 us (98%)
  between operations  1.29 us (1%)
    pallas_call x1, Pallas kernels, per_device(): pl.pallas_call(section_kernel, out_shape=[shape((ROWS, COLS, D), BF16), s...  88.2 us
    pallas_call x1, Pallas kernels, per_device(): pl.pallas_call(functools.partial(finish_kernel, norm_scale, table_rows),...  5.39 us

profile of v2, /device:TPU:1, one launch (start us, length us, event | category | flops | bytes accessed | tf_op | source)
XLA Modules:
  0.0 94.9 jit_solution(1483035233804760686)
XLA Ops:
  1.3 88.2 %section.1 = (bf16[4,256,512]{2,1,0:T(8,128)(2,1)}, bf16[2,256,2048]{2,1,0:T(8,128)(2,1)}, f32[2,2,16,512]{3,2,1,0:T(8,128)}) custom-call(bf16[4,256,512]{2,1,0:T(8,128)(2,1)} %bitcast.4, bf16[4,256,512]{2,1,0:T(8,128)(2,1)} %bitcast.5, f32[3,3,512]{2,1,0:T(4,128)} %ck.1, s32[1]{0:T(128)S(6)} %copy.12.lead_index, f32[721,2,512]{2,1,0:T(2,128)} %cond_any.1, ...), custom_call_target="tpu_custom_call" | custom-call | tf_op jit(solution)/shard_map/section/pallas_call | solution.py:645
  89.5 5.4 %finish.1 = (f32[512,1536]{1,0:T(8,128)}, f32[512,512]{1,0:T(8,128)}, f32[3,3,512]{2,1,0:T(4,128)}, f32[721,2,512]{2,1,0:T(2,128)}, bf16[4,256,512]{2,1,0:T(8,128)(2,1)}) custom-call(bf16[2,256,2048]{2,1,0:T(8,128)(2,1)} %get-tuple-element.13.total, f32[4,16,512]{2,1,0:T(8,128)} %bitcast.6, bf16[4,256,512]{2,1,0:T(8,128)(2,1)} %get-tuple-element.15.gx), custom_call_target="tpu_custom_call" | custom-call | tf_op jit(solution)/shard_map/finish/pallas_call | solution.py:721

commit v3 on v2

--- a/solution.py
+++ b/solution.py
@@ -519,8 +519,10 @@
             xp[ROWS + 1, 8 : COLS + 8, :] = halo[1].astype(F32)
             lax.fori_loop(0, 2, edge_row, 0)
 
-        dn[r] = normed_back(dp, wqkv, i)
-        send(dn, dr, dsem, r)
+        @pl.when(i < 3)
+        def _():
+            dn[r] = normed_back(dp, wqkv, i)
+            send(dn, dr, dsem, r)
 
         @pl.when(i < 2)
         def _():
@@ -535,8 +537,10 @@
     for n in range(4):
         cols = slice(n * D, (n + 1) * D)
         grads[:, cols] = (acc[1 - core, :, cols] + grads_of(xg, cg, att, dp, late, theirs, n)).astype(BF16)
-    for part in range(NP):
-        swap(part).start()
+        if n > 0:
+            swap(n - 1).start()
+    dn[3] = normed_back(dp, wqkv, 3)
+    send(dn, dr, dsem, 3)
     for n in range(4):
         acc[core, :, n * D : (n + 1) * D] += grads_of(xg, cg, att, dp, late, ours, n)
     back_row(0)

time: 95.1 us -> 95.2 us (level)
  no operation moved by 1% of the time
where the time goes in v3:
time: 95.2 us; the launch traced here: 95 us
  Pallas kernels  93.7 us (98%)
  between operations  1.29 us (1%)
    pallas_call x1, Pallas kernels, per_device(): pl.pallas_call(section_kernel, out_shape=[shape((ROWS, COLS, D), BF16), s...  88.3 us
    pallas_call x1, Pallas kernels, per_device(): pl.pallas_call(functools.partial(finish_kernel, norm_scale, table_rows),...  5.41 us

profile of v3, /device:TPU:1, one launch (start us, length us, event | category | flops | bytes accessed | tf_op | source)
XLA Modules:
  0.0 95.0 jit_solution(11067593954739077212)
XLA Ops:
  1.3 88.3 %section.1 = (bf16[4,256,512]{2,1,0:T(8,128)(2,1)}, bf16[2,256,2048]{2,1,0:T(8,128)(2,1)}, f32[2,2,16,512]{3,2,1,0:T(8,128)}) custom-call(bf16[4,256,512]{2,1,0:T(8,128)(2,1)} %bitcast.4, bf16[4,256,512]{2,1,0:T(8,128)(2,1)} %bitcast.5, f32[3,3,512]{2,1,0:T(4,128)} %ck.1, s32[1]{0:T(128)S(6)} %copy.12.lead_index, f32[721,2,512]{2,1,0:T(2,128)} %cond_any.1, ...), custom_call_target="tpu_custom_call" | custom-call | tf_op jit(solution)/shard_map/section/pallas_call | solution.py:649
  89.6 5.4 %finish.1 = (f32[512,1536]{1,0:T(8,128)}, f32[512,512]{1,0:T(8,128)}, f32[3,3,512]{2,1,0:T(4,128)}, f32[721,2,512]{2,1,0:T(2,128)}, bf16[4,256,512]{2,1,0:T(8,128)(2,1)}) custom-call(bf16[2,256,2048]{2,1,0:T(8,128)(2,1)} %get-tuple-element.13.total, f32[4,16,512]{2,1,0:T(8,128)} %bitcast.6, bf16[4,256,512]{2,1,0:T(8,128)(2,1)} %get-tuple-element.15.gx), custom_call_target="tpu_custom_call" | custom-call | tf_op jit(solution)/shard_map/finish/pallas_call | solution.py:725
